TPU v7x, 512 devices: a whole 4x8x8 slice. The times are simulated.
512 devices in a mesh: tmpl: 32 (over x, y_hi, core), stn: 16 (over y_lo, z).
Axes of the slice: x: 4, y: 8 (y_hi: 4, y_lo: 2; y = y_hi * 2 + y_lo), z: 8, core: 2. Of those that a mesh axis runs over, the one named last changes fastest.
Arguments:
- data: bfloat16 [2, 96, 3, 1024], P(None, 'stn', None, 'tmpl'), may hold values from -6 to 6
- waves: bfloat16 [96, 512, 3, 300], P('stn', 'tmpl'), may hold values from -6 to 6
- slot_group: int32 [96, 512, 1], P('stn', 'tmpl'), may hold values from 0 to 31; in each aligned block of 16 rows (0 to 15, 16 to 31, ..., all dimensions but the last counted through in order) at most 2 rows name the same one
- slot_local: int32 [96, 512], P('stn', 'tmpl'), may hold values from 0 to 255
- moveout: int32 [96, 512], P('stn', 'tmpl'), may hold values from 0 to 469
- chan_mask: int32 [96, 3], P('stn'), may hold values 0 or 1
Outputs:
- scores: float32 [2, 8192, 256], P(None, ('tmpl', 'stn'))
Inputs may be any that keep to these rules, and one draw needn't show every extreme that they name: `slot_group`: among the 16 slots k*16 to (k+1)*16 - 1 of one station, no template group is named more than 2 times.
All inputs are finite; a program needn't handle non-finite values. No bound on the sum of `chan_mask` on one device may be relied on, other than what follows from the above.
Results may differ from a plain program's by a relative error of at most 0.0029.
Values may be sent and summed in bfloat16 or wider, within the bound.
A program may use at most 128 MiB of HBM per device.

v0:
```python
import jax
import jax.numpy as jnp
from jax import lax
from jax.sharding import PartitionSpec as P

NK = 256
TPD = 16
epsilon = 1e-06


def hankel(series, tap_count, lag_count):
    width = series.shape[-1]
    repeats = (1,) * (series.ndim - 1) + (tap_count + 1,)
    tiled = jnp.tile(series, repeats)[..., : tap_count * (width + 1)]
    return tiled.reshape(series.shape[:-1] + (tap_count, width + 1))[..., :lag_count]


def shift_rows(values, offsets):
    lag_index = offsets[..., None] + jnp.arange(NK, dtype=jnp.int32)
    return jnp.take_along_axis(values, lag_index, axis=-1)


def body(data, waves, slot_group, slot_local, moveout, chan_mask):
    samples = lax.all_gather(data, "tmpl", axis=3, tiled=True)
    blocks, stations_here, components, width = samples.shape
    slots = waves.shape[1]
    tap_count = waves.shape[3]
    lag_count = width - tap_count + 1
    tmpl_count = lax.axis_size("tmpl")
    slot_most = max(2, 2 * slots // tmpl_count)
    capacity = stations_here * slot_most
    slot_total = tmpl_count * capacity
    per_group = TPD * lax.axis_size("stn")
    group_size = 2
    group_count = stations_here // group_size
    stacked_data = jnp.moveaxis(
        samples.reshape(blocks, group_count, group_size, components, width), 1, 0
    )
    stacked_waves = waves.reshape(group_count, group_size, slots, components, tap_count)
    stacked_mask = chan_mask.reshape(group_count, group_size, components).astype(jnp.float32)

    def correlate(inputs):
        station_data, station_waves, station_mask = inputs
        hankel_rows = hankel(station_data, tap_count, lag_count)
        squares = station_data.astype(jnp.float32) ** 2
        running = jnp.cumsum(squares, axis=-1)
        padded = jnp.concatenate(
            [jnp.zeros(running.shape[:-1] + (1,), jnp.float32), running], axis=-1
        )
        data_power = (
            padded[..., tap_count : tap_count + lag_count] - padded[..., :lag_count]
        ) / tap_count
        wave_power = (
            jnp.einsum(
                "spcj,spcj->spc", station_waves, station_waves, preferred_element_type=jnp.float32
            )
            / tap_count
        )
        numerator = jnp.einsum(
            "spcj,bscjk->spbck", station_waves, hankel_rows, preferred_element_type=jnp.float32
        )
        denominator = (
            tap_count
            * jnp.sqrt(wave_power + epsilon)[:, :, None, :, None]
            * jnp.sqrt(jnp.moveaxis(data_power, 0, 1) + epsilon)[:, None]
        )
        channel_sum = jnp.sum(
            numerator / denominator * station_mask[:, None, None, :, None], axis=3
        )
        scaled = channel_sum / jnp.maximum(jnp.sum(station_mask, axis=-1), 1.0)[:, None, None, None]
        return scaled.astype(jnp.bfloat16)

    row_count = stations_here * slots
    corr_rows = lax.map(correlate, (stacked_data, stacked_waves, stacked_mask)).reshape(
        row_count, blocks, lag_count
    )
    group_ids = slot_group[..., 0]
    same_group = group_ids[:, :, None] == group_ids[:, None, :]
    earlier = jnp.arange(slots)[None, :] < jnp.arange(slots)[:, None]
    slot_rank = jnp.sum((same_group & earlier[None]).astype(jnp.int32), axis=2)
    position = (
        group_ids * capacity
        + jnp.arange(stations_here, dtype=jnp.int32)[:, None] * slot_most
        + slot_rank
    ).reshape(row_count)
    local_ids = slot_local.reshape(row_count)
    shift_by = moveout.reshape(row_count)
    id_rows = jnp.full((slot_total,), -1, jnp.int32).at[position].set(local_ids)
    id_rows = jnp.broadcast_to(
        id_rows.reshape(tmpl_count, capacity, 1), (tmpl_count, capacity, blocks)
    )
    template_axis = jnp.arange(per_group, dtype=jnp.int32)
    offsets = jnp.broadcast_to(shift_by[:, None], (row_count, blocks))
    shifted = shift_rows(corr_rows, offsets)
    send_rows = jnp.zeros((slot_total, blocks, NK), jnp.bfloat16).at[position].set(shifted)
    send_rows = send_rows.reshape(tmpl_count, capacity, blocks, NK)
    values = lax.all_to_all(send_rows, "tmpl", split_axis=0, concat_axis=0, tiled=True)
    template_ids = lax.all_to_all(id_rows, "tmpl", split_axis=0, concat_axis=0, tiled=True)
    items = values.shape[2]
    accumulate_template_ids = template_ids.reshape(slot_total, items)
    onehot = (
        jnp.transpose(accumulate_template_ids)[:, None, :] == template_axis[None, :, None]
    ).astype(jnp.bfloat16)
    stack_sums = jnp.einsum(
        "btq,qbk->btk",
        onehot,
        values.reshape(slot_total, items, NK),
        preferred_element_type=jnp.float32,
    )
    counts = jnp.sum(onehot, axis=2, dtype=jnp.float32)
    stack_sums, counts = (stack_sums, counts)
    owned_sums, owned_counts = (
        lax.psum_scatter(stack_sums, "stn", scatter_dimension=1, tiled=True),
        lax.psum_scatter(counts, "stn", scatter_dimension=1, tiled=True),
    )
    return (
        jnp.sqrt(jnp.float32(tap_count))
        * owned_sums
        / jnp.sqrt(jnp.maximum(owned_counts, 1.0))[..., None]
    )


def solution(mesh):
    in_specs = (
        P(None, "stn", None, "tmpl"),
        P("stn", "tmpl", None, None),
        P("stn", "tmpl", None),
        P("stn", "tmpl"),
        P("stn", "tmpl"),
        P("stn", None),
    )
    out_specs = P(None, ("tmpl", "stn"), None)
    return jax.shard_map(body, mesh=mesh, in_specs=in_specs, out_specs=out_specs, check_vma=False)
```

profile of v0, /device:TPU:4, one launch (start us, length us, event | category | flops | bytes accessed | tf_op | source)
XLA Modules:
  0.0 874.6 jit_solution(11526672355706711706)
XLA Ops:
  10.9 10.2 %all-to-all-start = ((s32[32,12,2]{1,2,0:T(2,128)}), s32[32,12,2]{1,2,0:T(2,128)S(1)}, u32[]{:S(2)}, u32[]{:S(2)}) async-start(s32[32,12,2]{1,2,0:T(2,128)} %broadcast_in_dim.21), calls=%async_computation | async-start | bytes 65536 | tf_op jit(solution)/shard_map/all_to_all | solution.py:98
  23.2 43.7 %all_gather.3 = bf16[2,6,3,1024]{1,0,2,3:T(2,128)(2,1)S(1)} all-gather(bf16[2,6,3,32]{1,0,2,3:T(2,128)(2,1)S(1)} %copy.41), channel_id=1, replica_groups=mesh['tmpl'=32,'stn'=16] {'tmpl'}, dimensions={3}, use_global_device_ids=true | all-gather | bytes 76032 | tf_op jit(solution)/shard_map/all_gather | solution.py:24
  66.9 2.1 copy.42
  69.8 152.6 %while.10 = (s32[]{:T(128)}, bf16[3,2,16,2,725]{4,3,2,1,0:T(2,128)(2,1)S(1)}, bf16[3,2,2,3,1024]{4,1,3,2,0:T(2,128)(2,1)S(1)}, bf16[3,2,16,3,300]{4,2,3,1,0:T(8,...) while((s32[]{:T(128)}, bf16[3,2,16,2,725]{4,3,2,1,0:T(2,128)(2,1)S(1)}, ...), condition=%wide.region_7.8_spmd, body=%wide.region_2.0_spmd.sunk | while | flops 85834096 | bytes 59822800 | solution.py:74
  69.9 3.4 reduce-window.12
  73.5 1.1 reduce-window.13
  75.0 3.9 tile.13
  78.9 9.1 %tile.14 = bf16[2,2,3,308224]{3,1,2,0:T(2,128)(2,1)} reshape(bf16[2,2,3,301,1024]{4,3,1,2,0:T(8,128)(2,1)} %tile.13) | data formatting | bytes 14794752 | tf_op jit(solution)/shard_map/while/body/eval_jaxpr/tile | solution.py:14
  88.0 7.4 slice.48
  95.5 21.2 %reshape.187 = bf16[2,2,3,300,1025]{4,3,1,2,0:T(8,128)(2,1)} reshape(bf16[2,2,3,307500]{3,1,2,0:T(2,128)(2,1)} %slice.48) | data formatting | bytes 14760000 | tf_op jit(solution)/shard_map/while/body/eval_jaxpr/reshape | solution.py:15
  116.9 3.5 fusion.47
  120.8 3.4 reduce-window.12
  124.4 1.1 reduce-window.13
  125.8 3.9 tile.13
  129.8 9.1 %tile.14 = bf16[2,2,3,308224]{3,1,2,0:T(2,128)(2,1)} reshape(bf16[2,2,3,301,1024]{4,3,1,2,0:T(8,128)(2,1)} %tile.13) | data formatting | bytes 14794752 | tf_op jit(solution)/shard_map/while/body/eval_jaxpr/tile | solution.py:14
  138.9 7.4 slice.48
  146.3 21.2 %reshape.187 = bf16[2,2,3,300,1025]{4,3,1,2,0:T(8,128)(2,1)} reshape(bf16[2,2,3,307500]{3,1,2,0:T(2,128)(2,1)} %slice.48) | data formatting | bytes 14760000 | tf_op jit(solution)/shard_map/while/body/eval_jaxpr/reshape | solution.py:15
  167.8 3.5 fusion.47
  171.7 3.4 reduce-window.12
  176.7 3.9 tile.13
  180.6 9.1 %tile.14 = bf16[2,2,3,308224]{3,1,2,0:T(2,128)(2,1)} reshape(bf16[2,2,3,301,1024]{4,3,1,2,0:T(8,128)(2,1)} %tile.13) | data formatting | bytes 14794752 | tf_op jit(solution)/shard_map/while/body/eval_jaxpr/tile | solution.py:14
  189.8 7.4 slice.48
  197.2 21.2 %reshape.187 = bf16[2,2,3,300,1025]{4,3,1,2,0:T(8,128)(2,1)} reshape(bf16[2,2,3,307500]{3,1,2,0:T(2,128)(2,1)} %slice.48) | data formatting | bytes 14760000 | tf_op jit(solution)/shard_map/while/body/eval_jaxpr/reshape | solution.py:15
  218.7 3.5 fusion.47
  222.4 466.6 %gather_fusion = bf16[49152]{0:T(1024)(128)(2,1)S(1)} fusion(bf16[96,2,725]{2,1,0:T(2,128)(2,1)S(1)} %bitcast.75, s32[49152]{0:T(1024)S(1)} %bitcast.76), kind=kCustom, calls=%fused_computation | custom fusion | bytes 786432 | tf_op jit(solution)/shard_map/jit(take_along_axis)/gather | solution.py:20
  690.3 10.8 %scatter_fusion = bf16[384,2,256]{2,1,0:T(2,128)(2,1)} fusion(bf16[384,2,256]{2,1,0:T(2,128)(2,1)} %broadcast_in_dim.22, s32[96]{0:T(128)S(1)} %fusion.33, bf16[96,2,256]{2,1,0:T(2,128)(2,1)S(1)} %and_select_fusion), kind=kCustom, calls=%fused_computation.2 | custom fusion | bytes 295296 | tf_op jit(solution)/shard_map/scatter | solution.py:95
  701.1 10.0 %all-to-all-start.1 = ((bf16[32,12,2,256]{3,2,1,0:T(2,128)(2,1)}), bf16[32,12,2,256]{3,2,1,0:T(2,128)(2,1)S(1)}, u32[]{:S(2)}, u32[]{:S(2)}) async-start(bf16[32,12,2,256]{3,2,1,0:T(2,128)(2,1)} %bitcast.15), calls=%async_computation.1 | async-start | bytes 786432 | tf_op jit(solution)/shard_map/all_to_all | solution.py:97
  712.4 11.7 %all-to-all-done.1 = bf16[32,12,2,256]{3,2,1,0:T(2,128)(2,1)S(1)} async-done(((bf16[32,12,2,256]{3,2,1,0:T(2,128)(2,1)}), bf16[32,12,2,256]{3,2,1,0:T(2,128)(2,1)S(1)}, u32[]{:S(2)}, u32[]{:S(2)}) %all-to-all-start.1) | async-done | bytes 393248 | tf_op jit(solution)/shard_map/all_to_all | solution.py:97
  724.1 1.1 fusion.24
  725.2 68.7 %reduce-scatter.7.cloned.1.call-done = f32[16,2]{1,0:T(8,128)} async-done(((f32[256,2]{1,0:T(8,128)}), f32[16,2]{1,0:T(8,128)}) %reduce-scatter.7.cloned.1.call-update) | async-done | bytes 144
  794.7 71.6 %reduce-scatter.5.cloned.1.call-done = f32[2,16,256]{2,1,0:T(8,128)} async-done(((f32[2,256,256]{2,1,0:T(8,128)}), f32[2,16,256]{2,1,0:T(8,128)}) %reduce-scatter.5.cloned.1.call-update) | async-done | bytes 32784 | tf_op jit(solution)/shard_map/reduce_scatter | solution.py:113
  866.3 1.4 multiply_divide_fusion
  (100 shorter events, 14.7 us)
Async XLA Ops:
  10.9 690.3 %all-to-all-start = ((s32[32,12,2]{1,2,0:T(2,128)}), s32[32,12,2]{1,2,0:T(2,128)S(1)}, u32[]{:S(2)}, u32[]{:S(2)}) async-start(s32[32,12,2]{1,2,0:T(2,128)} %broadcast_in_dim.21), calls=%async_computation | async-start | bytes 65536 | tf_op jit(solution)/shard_map/all_to_all | solution.py:98
  95.5 21.2 %copy-start = (bf16[3,2,16,3,300]{4,2,3,1,0:T(8,128)(2,1)S(1)}, bf16[3,2,16,3,300]{4,2,3,1,0:T(8,128)(2,1)}, u32[]{:S(2)}) copy-start(bf16[3,2,16,3,300]{4,2,3,1,0:T(8,128)(2,1)} %get-tuple-element.112) | copy-start | bytes 518404 | tf_op jit(solution)/shard_map/while
  146.3 21.2 %copy-start = (bf16[3,2,16,3,300]{4,2,3,1,0:T(8,128)(2,1)S(1)}, bf16[3,2,16,3,300]{4,2,3,1,0:T(8,128)(2,1)}, u32[]{:S(2)}) copy-start(bf16[3,2,16,3,300]{4,2,3,1,0:T(8,128)(2,1)} %get-tuple-element.112) | copy-start | bytes 518404 | tf_op jit(solution)/shard_map/while
  197.2 21.2 %copy-start = (bf16[3,2,16,3,300]{4,2,3,1,0:T(8,128)(2,1)S(1)}, bf16[3,2,16,3,300]{4,2,3,1,0:T(8,128)(2,1)}, u32[]{:S(2)}) copy-start(bf16[3,2,16,3,300]{4,2,3,1,0:T(8,128)(2,1)} %get-tuple-element.112) | copy-start | bytes 518404 | tf_op jit(solution)/shard_map/while
  701.1 22.9 %all-to-all-start.1 = ((bf16[32,12,2,256]{3,2,1,0:T(2,128)(2,1)}), bf16[32,12,2,256]{3,2,1,0:T(2,128)(2,1)S(1)}, u32[]{:S(2)}, u32[]{:S(2)}) async-start(bf16[32,12,2,256]{3,2,1,0:T(2,128)(2,1)} %bitcast.15), calls=%async_computation.1 | async-start | bytes 786432 | tf_op jit(solution)/shard_map/all_to_all | solution.py:97
  711.2 82.8 %reduce-scatter.7.cloned.1.call-start = ((), (), s32[]{:S(2)}) async-start(), calls=%async_computation.5 | async-start | bytes 139264
  712.3 154.0 %reduce-scatter.5.cloned.1.call-start = ((), (), s32[]{:S(2)}) async-start(), calls=%async_computation.4 | async-start | bytes 557056 | tf_op jit(solution)/shard_map/reduce_scatter | solution.py:113
Sparse Core Ops, SparseCore 0:
  714.8 79.0 reduce-scatter.6
  797.0 69.2 reduce-scatter.4
where the time goes:
time: 876 us; the launch traced here: 875 us
  local copies, waits for them, and re-layouts  614 us (70%)
  waiting for transfers between devices  152 us (17%)
  blocking collectives  43.7 us (5%)
  starting transfers between devices  20.4 us (2%)
  other arithmetic  19.1 us (2%)
  between operations  13.5 us (2%)
  matrix products  11.6 us (1%)
    gather x2, local copies, waits for them, and re-layouts, shift_rows(): return jnp.take_along_axis(values, lag_index, axis=-1)  467 us
    reduce_scatter x1, waiting for transfers between devices, body(): lax.psum_scatter(stack_sums, 'stn', scatter_dimension=1, tiled=True)  71.6 us
    unnamed x3, waiting for transfers between devices  68.8 us
    reshape x3, local copies, waits for them, and re-layouts, hankel(): tiled.reshape(series.shape[:-1] + (tap_count, width + 1))[..., :lag_count]  63.6 us
    all_gather x1, blocking collectives, body(): samples = lax.all_gather(data, 'tmpl', axis=3, tiled=True)  43.7 us
    another operation x6, local copies, waits for them, and re-layouts, hankel(): tiled = jnp.tile(series, repeats)[..., :tap_count * (width + 1)]  39.3 us
    slice x3, local copies, waits for them, and re-layouts, hankel(): tiled = jnp.tile(series, repeats)[..., :tap_count * (width + 1)]  22.3 us
  transfers between devices with their start and end apart: 4, of which 3 were waited for; matrix products, arithmetic and copies ran while one was open for 73% of the time, Pallas kernels for 0%

commit v1 on v0

--- a/solution.py
+++ b/solution.py
@@ -21,7 +21,9 @@
 
 
 def body(data, waves, slot_group, slot_local, moveout, chan_mask):
-    samples = lax.all_gather(data, "tmpl", axis=3, tiled=True)
+    samples = jnp.concatenate(
+        lax.all_to_all(jnp.stack([data] * lax.axis_size("tmpl")), "tmpl", 0, 0), axis=3
+    )
     blocks, stations_here, components, width = samples.shape
     slots = waves.shape[1]
     tap_count = waves.shape[3]

time: 876 us -> 840 us (0.959)
  the two profiles are of different devices: /device:TPU:4 before, /device:TPU:2 now
where the time goes in v1:
time: 840 us; the launch traced here: 838 us
  local copies, waits for them, and re-layouts  614 us (73%)
  waiting for transfers between devices  154 us (18%)
  starting transfers between devices  26.8 us (3%)
  other arithmetic  19.1 us (2%)
  between operations  13.6 us (2%)
  matrix products  11.6 us (1%)
    gather x2, local copies, waits for them, and re-layouts, shift_rows(): return jnp.take_along_axis(values, lag_index, axis=-1)  467 us
    reduce_scatter x1, waiting for transfers between devices, body(): lax.psum_scatter(stack_sums, 'stn', scatter_dimension=1, tiled=True)  71.6 us
    unnamed x3, waiting for transfers between devices  66.5 us
    reshape x3, local copies, waits for them, and re-layouts, hankel(): tiled.reshape(series.shape[:-1] + (tap_count, width + 1))[..., :lag_count]  63.6 us
    another operation x9, local copies, waits for them, and re-layouts, hankel(): tiled = jnp.tile(series, repeats)[..., :tap_count * (width + 1)]  39.3 us
    slice x3, local copies, waits for them, and re-layouts, hankel(): tiled = jnp.tile(series, repeats)[..., :tap_count * (width + 1)]  22.3 us
  transfers between devices with their start and end apart: 5, of which 4 were waited for; matrix products, arithmetic and copies ran while one was open for 76% of the time, Pallas kernels for 0%

profile of v1, /device:TPU:2, one launch (start us, length us, event | category | flops | bytes accessed | tf_op | source)
XLA Modules:
  0.0 838.5 jit_solution(6617366200517041592)
XLA Ops:
  8.3 10.3 %all-to-all-start.1 = ((bf16[32,2,576]{2,1,0:T(2,128)(2,1)}), bf16[32,2,576]{2,1,0:T(2,128)(2,1)S(1)}, u32[]{:S(2)}, u32[]{:S(2)}) async-start(bf16[32,2,576]{2,1,0:T(2,128)(2,1)} %reshape.188), calls=%async_computation.1 | async-start | bytes 163840 | tf_op jit(solution)/shard_map/all_to_all | solution.py:25
  24.3 3.1 all-to-all-done.1
  28.0 6.7 all-to-all-start
  35.6 152.5 %while.10 = (s32[]{:T(128)}, bf16[3,2,16,2,725]{4,3,2,1,0:T(2,128)(2,1)S(1)}, bf16[3,2,2,3,1024]{4,2,0,3,1:T(2,128)(2,1)S(1)}, bf16[3,2,16,3,300]{4,2,3,1,0:T(8,...) while((s32[]{:T(128)}, bf16[3,2,16,2,725]{4,3,2,1,0:T(2,128)(2,1)S(1)}, ...), condition=%wide.region_7.8_spmd, body=%wide.region_2.0_spmd.sunk | while | flops 85834096 | bytes 59773652 | solution.py:76
  35.7 3.4 reduce-window.12
  39.4 1.1 reduce-window.13
  40.8 3.9 tile.13
  44.7 9.1 %tile.14 = bf16[2,2,3,308224]{3,1,2,0:T(2,128)(2,1)} reshape(bf16[2,2,3,301,1024]{4,3,1,2,0:T(8,128)(2,1)} %tile.13) | data formatting | bytes 14794752 | tf_op jit(solution)/shard_map/while/body/eval_jaxpr/tile | solution.py:14
  53.9 7.4 slice.48
  61.3 21.2 %reshape.191 = bf16[2,2,3,300,1025]{4,3,1,2,0:T(8,128)(2,1)} reshape(bf16[2,2,3,307500]{3,1,2,0:T(2,128)(2,1)} %slice.48) | data formatting | bytes 14760000 | tf_op jit(solution)/shard_map/while/body/eval_jaxpr/reshape | solution.py:15
  82.7 3.5 fusion.47
  86.6 3.4 reduce-window.12
  90.2 1.1 reduce-window.13
  91.6 3.9 tile.13
  95.6 9.1 %tile.14 = bf16[2,2,3,308224]{3,1,2,0:T(2,128)(2,1)} reshape(bf16[2,2,3,301,1024]{4,3,1,2,0:T(8,128)(2,1)} %tile.13) | data formatting | bytes 14794752 | tf_op jit(solution)/shard_map/while/body/eval_jaxpr/tile | solution.py:14
  104.7 7.4 slice.48
  112.1 21.2 %reshape.191 = bf16[2,2,3,300,1025]{4,3,1,2,0:T(8,128)(2,1)} reshape(bf16[2,2,3,307500]{3,1,2,0:T(2,128)(2,1)} %slice.48) | data formatting | bytes 14760000 | tf_op jit(solution)/shard_map/while/body/eval_jaxpr/reshape | solution.py:15
  133.6 3.5 fusion.47
  137.4 3.4 reduce-window.12
  142.5 3.9 tile.13
  146.4 9.1 %tile.14 = bf16[2,2,3,308224]{3,1,2,0:T(2,128)(2,1)} reshape(bf16[2,2,3,301,1024]{4,3,1,2,0:T(8,128)(2,1)} %tile.13) | data formatting | bytes 14794752 | tf_op jit(solution)/shard_map/while/body/eval_jaxpr/tile | solution.py:14
  155.5 7.4 slice.48
  163.0 21.2 %reshape.191 = bf16[2,2,3,300,1025]{4,3,1,2,0:T(8,128)(2,1)} reshape(bf16[2,2,3,307500]{3,1,2,0:T(2,128)(2,1)} %slice.48) | data formatting | bytes 14760000 | tf_op jit(solution)/shard_map/while/body/eval_jaxpr/reshape | solution.py:15
  184.4 3.5 fusion.47
  188.1 466.6 %gather_fusion = bf16[49152]{0:T(1024)(128)(2,1)S(1)} fusion(bf16[96,2,725]{2,1,0:T(2,128)(2,1)S(1)} %bitcast.87, s32[49152]{0:T(1024)S(1)} %bitcast.88), kind=kCustom, calls=%fused_computation | custom fusion | bytes 786432 | tf_op jit(solution)/shard_map/jit(take_along_axis)/gather | solution.py:20
  656.1 10.8 %scatter_fusion = bf16[384,2,256]{2,1,0:T(2,128)(2,1)} fusion(bf16[384,2,256]{2,1,0:T(2,128)(2,1)} %broadcast_in_dim.22, s32[96]{0:T(128)S(1)} %fusion.33, bf16[96,2,256]{2,1,0:T(2,128)(2,1)S(1)} %and_select_fusion), kind=kCustom, calls=%fused_computation.2 | custom fusion | bytes 295296 | tf_op jit(solution)/shard_map/scatter | solution.py:97
  666.9 9.8 %all-to-all-start.2 = ((bf16[32,12,2,256]{3,2,1,0:T(2,128)(2,1)}), bf16[32,12,2,256]{3,2,1,0:T(2,128)(2,1)S(1)}, u32[]{:S(2)}, u32[]{:S(2)}) async-start(bf16[32,12,2,256]{3,2,1,0:T(2,128)(2,1)} %bitcast.15), calls=%async_computation.2 | async-start | bytes 786432 | tf_op jit(solution)/shard_map/all_to_all | solution.py:99
  677.9 12.3 %all-to-all-done.2 = bf16[32,12,2,256]{3,2,1,0:T(2,128)(2,1)S(1)} async-done(((bf16[32,12,2,256]{3,2,1,0:T(2,128)(2,1)}), bf16[32,12,2,256]{3,2,1,0:T(2,128)(2,1)S(1)}, u32[]{:S(2)}, u32[]{:S(2)}) %all-to-all-start.2) | async-done | bytes 393248 | tf_op jit(solution)/shard_map/all_to_all | solution.py:99
  690.2 1.1 fusion.24
  691.3 66.5 %reduce-scatter.7.cloned.1.call-done = f32[16,2]{1,0:T(8,128)} async-done(((f32[256,2]{1,0:T(8,128)}), f32[16,2]{1,0:T(8,128)}) %reduce-scatter.7.cloned.1.call-update) | async-done | bytes 144
  758.6 71.6 %reduce-scatter.5.cloned.1.call-done = f32[2,16,256]{2,1,0:T(8,128)} async-done(((f32[2,256,256]{2,1,0:T(8,128)}), f32[2,16,256]{2,1,0:T(8,128)}) %reduce-scatter.5.cloned.1.call-update) | async-done | bytes 32784 | tf_op jit(solution)/shard_map/reduce_scatter | solution.py:115
  830.2 1.4 multiply_divide_fusion
  (104 shorter events, 16.4 us)
Async XLA Ops:
  6.5 0.7 copy-start
  8.3 19.1 %all-to-all-start.1 = ((bf16[32,2,576]{2,1,0:T(2,128)(2,1)}), bf16[32,2,576]{2,1,0:T(2,128)(2,1)S(1)}, u32[]{:S(2)}, u32[]{:S(2)}) async-start(bf16[32,2,576]{2,1,0:T(2,128)(2,1)} %reshape.188), calls=%async_computation.1 | async-start | bytes 163840 | tf_op jit(solution)/shard_map/all_to_all | solution.py:25
  28.0 638.9 %all-to-all-start = ((s32[32,12,2]{1,2,0:T(2,128)}), s32[32,12,2]{1,2,0:T(2,128)S(1)}, u32[]{:S(2)}, u32[]{:S(2)}) async-start(s32[32,12,2]{1,2,0:T(2,128)} %broadcast_in_dim.21), calls=%async_computation | async-start | bytes 65536 | tf_op jit(solution)/shard_map/all_to_all | solution.py:100
  61.3 21.2 %copy-start.1 = (bf16[3,2,16,3,300]{4,2,3,1,0:T(8,128)(2,1)S(1)}, bf16[3,2,16,3,300]{4,2,3,1,0:T(8,128)(2,1)}, u32[]{:S(2)}) copy-start(bf16[3,2,16,3,300]{4,2,3,1,0:T(8,128)(2,1)} %get-tuple-element.117) | copy-start | bytes 518404 | tf_op jit(solution)/shard_map/while
  112.1 21.2 %copy-start.1 = (bf16[3,2,16,3,300]{4,2,3,1,0:T(8,128)(2,1)S(1)}, bf16[3,2,16,3,300]{4,2,3,1,0:T(8,128)(2,1)}, u32[]{:S(2)}) copy-start(bf16[3,2,16,3,300]{4,2,3,1,0:T(8,128)(2,1)} %get-tuple-element.117) | copy-start | bytes 518404 | tf_op jit(solution)/shard_map/while
  163.0 21.2 %copy-start.1 = (bf16[3,2,16,3,300]{4,2,3,1,0:T(8,128)(2,1)S(1)}, bf16[3,2,16,3,300]{4,2,3,1,0:T(8,128)(2,1)}, u32[]{:S(2)}) copy-start(bf16[3,2,16,3,300]{4,2,3,1,0:T(8,128)(2,1)} %get-tuple-element.117) | copy-start | bytes 518404 | tf_op jit(solution)/shard_map/while
  666.9 23.3 %all-to-all-start.2 = ((bf16[32,12,2,256]{3,2,1,0:T(2,128)(2,1)}), bf16[32,12,2,256]{3,2,1,0:T(2,128)(2,1)S(1)}, u32[]{:S(2)}, u32[]{:S(2)}) async-start(bf16[32,12,2,256]{3,2,1,0:T(2,128)(2,1)} %bitcast.15), calls=%async_computation.2 | async-start | bytes 786432 | tf_op jit(solution)/shard_map/all_to_all | solution.py:99
  676.7 81.1 %reduce-scatter.7.cloned.1.call-start = ((), (), s32[]{:S(2)}) async-start(), calls=%async_computation.6 | async-start | bytes 139264
  677.9 152.3 %reduce-scatter.5.cloned.1.call-start = ((), (), s32[]{:S(2)}) async-start(), calls=%async_computation.5 | async-start | bytes 557056 | tf_op jit(solution)/shard_map/reduce_scatter | solution.py:115
Sparse Core Ops, SparseCore 0:
  680.3 77.4 reduce-scatter.6
  760.8 69.3 reduce-scatter.4
